TPU v7x, 256 devices: a whole 4x4x8 slice. The times are simulated.
256 devices in a mesh: con: 16 (over z_hi, x, core), res: 16 (over y, z_lo).
Axes of the slice: x: 4, y: 4, z: 8 (z_hi: 2, z_lo: 4; z = z_hi * 4 + z_lo), core: 2. Of those that a mesh axis runs over, the one named last changes fastest.
Arguments:
- integrals: float32 [24576, 24576], P('res', 'con'), as said below
- tile_mask: int32 [96, 96], P('res', 'con'), may hold values from 0 to 1, as said below
- amplitudes: float32 [24576, 384], P(('con', 'res')), may hold values from -4 to 4
- other_first: float32 [24576, 384], P(('res', 'con')), may hold values from -6 to 6
- other_second: float32 [24576, 384], P(('con', 'res')), may hold values from -6 to 6
- vir_index: int32 [2, 24576], replicated, may hold values from 0 to 1599
- occ_index: int32 [2, 384], replicated, may hold values from 0 to 31, as said below
- partner: int32 [384], replicated, may hold values from 0 to 383, as said below
- eps_vir: float32 [1600], replicated, may hold values from 0.2 to 3
- eps_occ: float32 [32], replicated, may hold values from -2 to -0.2
Outputs:
- first_update: float32 [24576, 384], P(('res', 'con'))
- second_update: float32 [24576, 384], P(('con', 'res'))
Inputs may be any that keep to these rules, and one draw needn't show every extreme that they name: integrals is symmetric: integrals[p, s] == integrals[s, p]. tile_mask is symmetric and its diagonal is 1. partner is a permutation that is its own inverse with no fixed point. The two orbitals of an occupied pair differ, and occ_index[0, partner[q]] == occ_index[1, q].
All inputs are finite; a program needn't handle non-finite values.
Results may differ from a plain program's by a relative error of at most 0.000065.
Values sent between devices are 32-bit elements; how exact they have to be, the bound alone decides.
A program may use at most 128 MiB of HBM per device.

v0:
```python
import jax
import jax.numpy as jnp
from jax import lax
from jax.sharding import PartitionSpec as P

W = 256
precise = lax.Precision.HIGHEST


def pair_energy(pair_index, table):
    orbitals = lax.broadcasted_iota(jnp.int32, (1, table.shape[0]), 1)
    counts = (pair_index[0][:, None] == orbitals).astype(jnp.float32) + (
        pair_index[1][:, None] == orbitals
    ).astype(jnp.float32)
    return jnp.dot(counts, table, precision=precise, preferred_element_type=jnp.float32)


def vir_energy_rows(vir_index, eps_vir, row_offset, row_count):
    picked = lax.dynamic_slice_in_dim(vir_index, row_offset, row_count, 1)
    block_rows = min(row_count, 512)
    blocks = picked.reshape(2, row_count // block_rows, block_rows).transpose(1, 0, 2)
    energies = lax.map(lambda part_index: pair_energy(part_index, eps_vir), blocks)
    return energies.reshape(row_count)


def renew(ladder, other, vir_rows, occ_energy, swap_matrix):
    unscaled = (other + ladder) / (vir_rows[:, None] - occ_energy[None, :])
    swapped = jnp.dot(unscaled, swap_matrix, precision=precise, preferred_element_type=jnp.float32)
    return 0.5 * (unscaled - swapped)


def per_device(
    integrals,
    tile_mask,
    amplitudes,
    other_first,
    other_second,
    vir_index,
    occ_index,
    partner,
    eps_vir,
    eps_occ,
):
    row_count, col_count = integrals.shape
    tiles_down, tiles_across = tile_mask.shape
    weights = tile_mask.astype(jnp.float32)
    screened = (
        integrals.reshape(tiles_down, W, tiles_across, W) * weights[:, None, :, None]
    ).reshape(row_count, col_count)
    occ_energy = pair_energy(occ_index, eps_occ)
    occ_cols = amplitudes.shape[1]
    column_ids = lax.broadcasted_iota(jnp.int32, (occ_cols, occ_cols), 0)
    swap_matrix = (column_ids == partner[None, :]).astype(jnp.float32)
    n_con = lax.axis_size("con")
    n_res = lax.axis_size("res")
    con_at = lax.axis_index("con")
    res_at = lax.axis_index("res")
    fine_rows = amplitudes.shape[0]
    partial_one = jnp.dot(
        screened,
        lax.all_gather(amplitudes, "res", axis=0, tiled=True),
        precision=precise,
        preferred_element_type=jnp.float32,
    )
    ladder_one = lax.psum_scatter(partial_one, "con", scatter_dimension=0, tiled=True)
    first_offset = (res_at * n_con + con_at) * fine_rows
    first_vir = vir_energy_rows(vir_index, eps_vir, first_offset, fine_rows)
    first_update = renew(ladder_one, other_first, first_vir, occ_energy, swap_matrix)
    partial_two = lax.dot_general(
        screened,
        lax.all_gather(first_update, "con", axis=0, tiled=True),
        (((0,), (0,)), ((), ())),
        precision=precise,
        preferred_element_type=jnp.float32,
    )
    ladder_two = lax.psum_scatter(partial_two, "res", scatter_dimension=0, tiled=True)
    second_offset = (con_at * n_res + res_at) * fine_rows
    second_vir = vir_energy_rows(vir_index, eps_vir, second_offset, fine_rows)
    second_update = renew(ladder_two, other_second, second_vir, occ_energy, swap_matrix)
    return (first_update, second_update)


def solution(mesh):
    return jax.shard_map(
        per_device,
        mesh=mesh,
        in_specs=(
            P("res", "con"),
            P("res", "con"),
            P(("con", "res"), None),
            P(("res", "con"), None),
            P(("con", "res"), None),
            P(),
            P(),
            P(),
            P(),
            P(),
        ),
        out_specs=(P(("res", "con"), None), P(("con", "res"), None)),
        check_vma=False,
    )
```

profile of v0, /device:TPU:2, one launch (start us, length us, event | category | flops | bytes accessed | tf_op | source)
XLA Modules:
  0.0 389.8 jit_solution(10868963700371033135)
XLA Ops:
  7.2 0.0 all-gather.3.cloned.1.call-start
  7.2 0.7 all-gather.3.cloned.1.call-update
  7.9 0.0 reduce-scatter.3.cloned.1.call-start
  8.0 0.7 convert_element_type.26
  8.7 0.9 mul.29
  9.5 8.4 %copy.12 = f32[192,8,6,256]{3,1,2,0:T(8,128)} copy(f32[192,8,6,256]{3,2,1,0:T(8,128)S(1)} %bitcast.24) | data formatting | bytes 18874368
  17.9 12.2 %mul.31 = f32[1536,1536]{1,0:T(8,128)} multiply(f32[1536,1536]{1,0:T(8,128)} %param.10, f32[1536,1536]{1,0:T(8,128)} %bitcast.25) | non-fusion elementwise | flops 2359296 | bytes 28311552 | tf_op jit(solution)/shard_map/mul | solution.py:48
  30.1 71.9 %all-gather.3.cloned.1.call-done = f32[1536,384]{1,0:T(8,128)} async-done(((f32[96,384]{1,0:T(8,128)}), f32[1536,384]{1,0:T(8,128)}) %all-gather.3.cloned.1.call-update) | async-done | bytes 2359312 | tf_op jit(solution)/shard_map/all_gather | solution.py:61
  101.9 18.8 %fusion.30 = f32[1536,384]{1,0:T(8,128)} fusion(f32[1536,1536]{1,0:T(8,128)} %mul.31, f32[1536,384]{1,0:T(8,128)} %all-gather.3.cloned.1.call-done), kind=kOutput, calls=%fused_computation.50 | convolution fusion | flops 10871635968 | bytes 14155776 | tf_op jit(solution)/shard_map/dot_general | solution.py:59
  120.8 0.0 reduce-scatter.3.cloned.1.call-update
  120.8 0.2 all-gather.5.cloned.1.call-start
  121.1 0.4 copy-done.1
  121.5 0.8 constant_dynamic-slice_fusion
  122.3 0.5 convolution_reduce_fusion
  122.8 0.8 convolution_bitcast_fusion.1
  123.6 84.8 %reduce-scatter.3.cloned.1.call-done = f32[96,384]{1,0:T(8,128)} async-done(((f32[1536,384]{1,0:T(8,128)}), f32[96,384]{1,0:T(8,128)}) %reduce-scatter.3.cloned.1.call-update) | async-done | bytes 147472 | tf_op jit(solution)/shard_map/reduce_scatter | solution.py:65
  208.4 2.0 fusion
  210.4 0.0 reduce-scatter.5.cloned.1.call-start
  210.4 62.1 %all-gather.5.cloned.1.call-done = f32[1536,384]{1,0:T(8,128)} async-done(((f32[96,384]{1,0:T(8,128)}), f32[1536,384]{1,0:T(8,128)}) %all-gather.5.cloned.1.call-update) | async-done | bytes 2359312 | tf_op jit(solution)/shard_map/all_gather | solution.py:71
  272.5 19.1 %fusion.31 = f32[1536,384]{1,0:T(8,128)} fusion(f32[1536,1536]{1,0:T(8,128)} %mul.31, f32[1536,384]{1,0:T(8,128)} %all-gather.5.cloned.1.call-done), kind=kOutput, calls=%fused_computation.51 | convolution fusion | flops 10871635968 | bytes 14155776 | tf_op jit(solution)/shard_map/dot_general | solution.py:69
  291.6 0.0 reduce-scatter.5.cloned.1.call-update
  291.7 0.8 convolution_bitcast_fusion
  292.5 88.8 %reduce-scatter.5.cloned.1.call-done = f32[96,384]{1,0:T(8,128)} async-done(((f32[1536,384]{1,0:T(8,128)}), f32[96,384]{1,0:T(8,128)}) %reduce-scatter.5.cloned.1.call-update) | async-done | bytes 147472 | tf_op jit(solution)/shard_map/reduce_scatter | solution.py:76
  381.3 2.0 fusion.1
  (15 shorter events, 0.1 us)
Async XLA Ops:
  7.2 115.1 %copy-start = (f32[32]{0:T(128)S(1)}, f32[32]{0:T(128)}, u32[]{:S(2)}) copy-start(f32[32]{0:T(128)} %param.19) | copy-start | bytes 388
  7.2 94.8 %all-gather.3.cloned.1.call-start = ((), (), s32[]{:S(2)}) async-start(), calls=%async_computation.2 | async-start | bytes 2506752 | tf_op jit(solution)/shard_map/all_gather | solution.py:61
  7.9 200.5 %reduce-scatter.3.cloned.1.call-start = ((), (), s32[]{:S(2)}) async-start(), calls=%async_computation.3 | async-start | bytes 2506752 | tf_op jit(solution)/shard_map/reduce_scatter | solution.py:65
  120.8 0.7 copy-start.1
  120.8 1.5 copy-start.2
  120.8 87.6 %copy-start.3 = (f32[96,384]{1,0:T(8,128)S(1)}, f32[96,384]{1,0:T(8,128)}, u32[]{:S(2)}) copy-start(f32[96,384]{1,0:T(8,128)} %param.13) | copy-start | bytes 442372
  120.8 87.6 %copy-start.5 = (s32[384]{0:T(512)S(1)}, s32[384]{0:T(512)}, u32[]{:S(2)}) copy-start(s32[384]{0:T(512)} %param.17) | copy-start | bytes 4612
  120.8 151.7 %all-gather.5.cloned.1.call-start = ((), (), s32[]{:S(2)}) async-start(), calls=%async_computation.4 | async-start | bytes 2506752 | tf_op jit(solution)/shard_map/all_gather | solution.py:71
  210.4 170.9 %reduce-scatter.5.cloned.1.call-start = ((), (), s32[]{:S(2)}) async-start(), calls=%async_computation.5 | async-start | bytes 2506752 | tf_op jit(solution)/shard_map/reduce_scatter | solution.py:76
  291.6 89.7 %copy-start.4 = (f32[96,384]{1,0:T(8,128)S(1)}, f32[96,384]{1,0:T(8,128)}, u32[]{:S(2)}) copy-start(f32[96,384]{1,0:T(8,128)} %param.14) | copy-start | bytes 442372
Sparse Core Ops, SparseCore 0:
  9.8 92.0 all-gather.2
  120.9 87.3 reduce-scatter.2
  211.7 60.7 all-gather.4
  291.8 89.4 reduce-scatter.4
where the time goes:
time: 390 us
  waiting for transfers between devices  308 us (79%)
  matrix products  44 us (11%)
  between operations  13.8 us (4%)
  other arithmetic  12.9 us (3%)
  local copies, waits for them, and re-layouts  10.5 us (3%)
    reduce_scatter x1, waiting for transfers between devices, per_device(): lax.psum_scatter(partial_two, 'res', scatter_dimension=0, tiled=True)  88.8 us
    reduce_scatter x1, waiting for transfers between devices, per_device(): lax.psum_scatter(partial_one, 'con', scatter_dimension=0, tiled=True)  84.8 us
    all_gather x1, waiting for transfers between devices, per_device(): lax.all_gather(amplitudes, 'res', axis=0, tiled=True)  71.9 us
    all_gather x1, waiting for transfers between devices, per_device(): lax.all_gather(first_update, 'con', axis=0, tiled=True)  62.1 us
    dot_general x1, matrix products, per_device(): lax.dot_general(screened, lax.all_gather(first_update, 'con', axis=0, til...  19.1 us
    dot_general x1, matrix products, per_device(): jnp.dot(screened, lax.all_gather(amplitudes, 'res', axis=0, tiled=True),...  18.8 us
    mul x1, other arithmetic, per_device(): integrals.reshape(tiles_down, W, tiles_across, W)  12.2 us
    unnamed x14, local copies, waits for them, and re-layouts  8.81 us
  transfers between devices with their start and end apart: 4, of which 4 were waited for; matrix products, arithmetic and copies ran while one was open for 6% of the time, Pallas kernels for 0%

commit v1 on v0

--- a/solution.py
+++ b/solution.py
@@ -56,11 +56,15 @@
     con_at = lax.axis_index("con")
     res_at = lax.axis_index("res")
     fine_rows = amplitudes.shape[0]
+
+    def sizes_raise(load, dim_i):
+        t1 = lax.axis_size("res")
+        v_next = jnp.stack(t1 * [load])
+        current_block = lax.all_to_all(v_next, axis_name="res", split_axis=0, concat_axis=0)
+        return jnp.concatenate(current_block, dim_i)
+
     partial_one = jnp.dot(
-        screened,
-        lax.all_gather(amplitudes, "res", axis=0, tiled=True),
-        precision=precise,
-        preferred_element_type=jnp.float32,
+        screened, sizes_raise(amplitudes, 0), precision=precise, preferred_element_type=jnp.float32
     )
     ladder_one = lax.psum_scatter(partial_one, "con", scatter_dimension=0, tiled=True)
     first_offset = (res_at * n_con + con_at) * fine_rows

time: 390 us -> 363 us (0.931)
  waiting for transfers between devices: 308 us -> 270 us
  starting transfers between devices: 0.34 us -> 9.12 us
    all_gather x1 -> x0, waiting for transfers between devices: 71.9 us -> none  [per_device(): lax.all_gather(amplitudes, 'res', axis=0, tiled=True)]
    all_to_all x0 -> x1, waiting for transfers between devices: none -> 34.5 us  [sizes_raise(): lax.all_to_all(v_next, axis_name='res', split_axis=0, concat_axis=0)]
    all_to_all x0 -> x1, starting transfers between devices: none -> 8.81 us  [sizes_raise(): lax.all_to_all(v_next, axis_name='res', split_axis=0, concat_axis=0)]
    unnamed x14 -> x16, local copies, waits for them, and re-layouts: 8.81 us -> 8.81 us
  transfers between devices with their start and end apart: 4 -> 4, of which waited for: 4 -> 4; matrix products, arithmetic and copies ran while one was open for 6% -> 7% of each run, Pallas kernels for 0% -> 0%
where the time goes in v1:
time: 363 us
  waiting for transfers between devices  270 us (74%)
  matrix products  44 us (12%)
  between operations  13.8 us (4%)
  local copies, waits for them, and re-layouts  13.1 us (4%)
  other arithmetic  12.2 us (3%)
  starting transfers between devices  9.12 us (3%)
    reduce_scatter x1, waiting for transfers between devices, per_device(): lax.psum_scatter(partial_two, 'res', scatter_dimension=0, tiled=True)  88.4 us
    reduce_scatter x1, waiting for transfers between devices, per_device(): lax.psum_scatter(partial_one, 'con', scatter_dimension=0, tiled=True)  85.3 us
    all_gather x1, waiting for transfers between devices, per_device(): lax.all_gather(first_update, 'con', axis=0, tiled=True)  62 us
    all_to_all x1, waiting for transfers between devices, sizes_raise(): lax.all_to_all(v_next, axis_name='res', split_axis=0, concat_axis=0)  34.5 us
    dot_general x1, matrix products, per_device(): lax.dot_general(screened, lax.all_gather(first_update, 'con', axis=0, til...  19.1 us
    dot_general x1, matrix products, per_device(): jnp.dot(screened, sizes_raise(amplitudes, 0), precision=precise, preferre...  18.8 us
    mul x1, other arithmetic, per_device(): integrals.reshape(tiles_down, W, tiles_across, W)  12.2 us
    all_to_all x1, starting transfers between devices, sizes_raise(): lax.all_to_all(v_next, axis_name='res', split_axis=0, concat_axis=0)  8.81 us
  transfers between devices with their start and end apart: 4, of which 4 were waited for; matrix products, arithmetic and copies ran while one was open for 7% of the time, Pallas kernels for 0%

profile of v1, /device:TPU:2, one launch (start us, length us, event | category | flops | bytes accessed | tf_op | source)
XLA Modules:
  0.0 362.6 jit_solution(10224527469894926557)
XLA Ops:
  7.2 2.6 stack.2
  9.8 8.8 %all-to-all-start = ((f32[16,96,384]{2,1,0:T(8,128)}), f32[16,96,384]{2,1,0:T(8,128)}, u32[]{:S(2)}, u32[]{:S(2)}) async-start(f32[16,96,384]{2,1,0:T(8,128)} %stack.2), calls=%async_computation | async-start | bytes 4718592 | tf_op jit(solution)/shard_map/all_to_all | solution.py:63
  18.6 0.0 reduce-scatter.3.cloned.1.call-start
  18.7 0.9 mul.29
  19.6 8.4 %copy.12 = f32[192,8,6,256]{3,1,2,0:T(8,128)} copy(f32[192,8,6,256]{3,2,1,0:T(8,128)S(1)} %bitcast.25) | data formatting | bytes 18874368
  27.9 12.2 %mul.31 = f32[1536,1536]{1,0:T(8,128)} multiply(f32[1536,1536]{1,0:T(8,128)} %param.10, f32[1536,1536]{1,0:T(8,128)} %bitcast.26) | non-fusion elementwise | flops 2359296 | bytes 28311552 | tf_op jit(solution)/shard_map/mul | solution.py:48
  40.1 34.5 %all-to-all-done = f32[16,96,384]{2,1,0:T(8,128)} async-done(((f32[16,96,384]{2,1,0:T(8,128)}), f32[16,96,384]{2,1,0:T(8,128)}, u32[]{:S(2)}, u32[]{:S(2)}) %all-to-all-start) | async-done | bytes 2359328 | tf_op jit(solution)/shard_map/all_to_all | solution.py:63
  74.6 18.8 %fusion.30 = f32[1536,384]{1,0:T(8,128)} fusion(f32[1536,1536]{1,0:T(8,128)} %mul.31, f32[1536,384]{1,0:T(8,128)} %bitcast), kind=kOutput, calls=%fused_computation.50 | convolution fusion | flops 10871635968 | bytes 14155776 | tf_op jit(solution)/shard_map/dot_general | solution.py:66
  93.5 0.0 reduce-scatter.3.cloned.1.call-update
  93.5 0.2 all-gather.2.cloned.1.call-start
  93.7 0.4 copy-done.1
  94.2 0.8 constant_dynamic-slice_fusion
  95.0 0.5 convolution_reduce_fusion
  95.4 0.8 convolution_bitcast_fusion.1
  96.2 85.3 %reduce-scatter.3.cloned.1.call-done = f32[96,384]{1,0:T(8,128)} async-done(((f32[1536,384]{1,0:T(8,128)}), f32[96,384]{1,0:T(8,128)}) %reduce-scatter.3.cloned.1.call-update) | async-done | bytes 147472 | tf_op jit(solution)/shard_map/reduce_scatter | solution.py:69
  181.6 2.0 fusion
  183.6 0.0 all-gather.2.cloned.1.call-update
  183.6 0.0 reduce-scatter.5.cloned.1.call-start
  183.6 62.0 %all-gather.2.cloned.1.call-done = f32[1536,384]{1,0:T(8,128)} async-done(((f32[96,384]{1,0:T(8,128)}), f32[1536,384]{1,0:T(8,128)}) %all-gather.2.cloned.1.call-update) | async-done | bytes 2359312 | tf_op jit(solution)/shard_map/all_gather | solution.py:75
  245.7 19.1 %fusion.31 = f32[1536,384]{1,0:T(8,128)} fusion(f32[1536,1536]{1,0:T(8,128)} %mul.31, f32[1536,384]{1,0:T(8,128)} %all-gather.2.cloned.1.call-done), kind=kOutput, calls=%fused_computation.51 | convolution fusion | flops 10871635968 | bytes 14155776 | tf_op jit(solution)/shard_map/dot_general | solution.py:73
  264.8 0.0 reduce-scatter.5.cloned.1.call-update
  264.8 0.8 convolution_bitcast_fusion
  265.6 88.4 %reduce-scatter.5.cloned.1.call-done = f32[96,384]{1,0:T(8,128)} async-done(((f32[1536,384]{1,0:T(8,128)}), f32[96,384]{1,0:T(8,128)}) %reduce-scatter.5.cloned.1.call-update) | async-done | bytes 147472 | tf_op jit(solution)/shard_map/reduce_scatter | solution.py:80
  354.1 2.0 fusion.1
  (17 shorter events, 0.1 us)
Async XLA Ops:
  7.2 87.8 %copy-start = (f32[32]{0:T(128)S(1)}, f32[32]{0:T(128)}, u32[]{:S(2)}) copy-start(f32[32]{0:T(128)} %param.19) | copy-start | bytes 388
  9.8 8.9 %copy-start.2 = (s32[6,6]{1,0:T(8,128)S(1)}, s32[6,6]{1,0:T(8,128)}, u32[]{:S(2)}) copy-start(s32[6,6]{1,0:T(8,128)} %param.11) | copy-start | bytes 436
  9.8 64.8 %all-to-all-start = ((f32[16,96,384]{2,1,0:T(8,128)}), f32[16,96,384]{2,1,0:T(8,128)}, u32[]{:S(2)}, u32[]{:S(2)}) async-start(f32[16,96,384]{2,1,0:T(8,128)} %stack.2), calls=%async_computation | async-start | bytes 4718592 | tf_op jit(solution)/shard_map/all_to_all | solution.py:63
  18.6 163.0 %reduce-scatter.3.cloned.1.call-start = ((), (), s32[]{:S(2)}) async-start(), calls=%async_computation.3 | async-start | bytes 2506752 | tf_op jit(solution)/shard_map/reduce_scatter | solution.py:69
  93.5 0.7 copy-start.1
  93.5 1.5 copy-start.3
  93.5 88.1 %copy-start.4 = (f32[96,384]{1,0:T(8,128)S(1)}, f32[96,384]{1,0:T(8,128)}, u32[]{:S(2)}) copy-start(f32[96,384]{1,0:T(8,128)} %param.13) | copy-start | bytes 442372
  93.5 88.1 %copy-start.6 = (s32[384]{0:T(512)S(1)}, s32[384]{0:T(512)}, u32[]{:S(2)}) copy-start(s32[384]{0:T(512)} %param.17) | copy-start | bytes 4612
  93.5 152.2 %all-gather.2.cloned.1.call-start = ((), (), s32[]{:S(2)}) async-start(), calls=%async_computation.4 | async-start | bytes 2506752 | tf_op jit(solution)/shard_map/all_gather | solution.py:75
  183.6 170.5 %reduce-scatter.5.cloned.1.call-start = ((), (), s32[]{:S(2)}) async-start(), calls=%async_computation.5 | async-start | bytes 2506752 | tf_op jit(solution)/shard_map/reduce_scatter | solution.py:80
  264.8 89.3 %copy-start.5 = (f32[96,384]{1,0:T(8,128)S(1)}, f32[96,384]{1,0:T(8,128)}, u32[]{:S(2)}) copy-start(f32[96,384]{1,0:T(8,128)} %param.14) | copy-start | bytes 442372
Sparse Core Ops, SparseCore 0:
  93.6 87.9 reduce-scatter.2
  184.9 60.7 all-gather.1
  265.0 89.0 reduce-scatter.4
